TPU v7x, 32 devices: a whole 2x2x4 slice. The times are simulated.
32 devices in a mesh: groups: 2 (over x), expert: 16 (over z, y, core).
Axes of the slice: x: 2, y: 2, z: 4, core: 2. Of those that a mesh axis runs over, the one named last changes fastest.
Arguments:
- tokens: bfloat16 [4096, 7168], P(('groups', 'expert')), parts along dimension 0, may hold values from -6 to 6
- route_ids: int32 [4096, 8], P(('groups', 'expert')), parts along dimension 0, may hold values from 0 to 255, as said below
- gate_fixed: int32 [4096, 8], P(('groups', 'expert')), parts along dimension 0, may hold values from 1 to 32767
- capacity: int32 [4], P('groups'), parts along dimension 0, may hold values from 1 to 2, as said below
- placement: int32 [2, 3], P('groups'), parts along dimension 0, may hold values from 0 to 1, as said below
- gate_weight: bfloat16 [16, 7168, 128], P('expert'), may hold values from -0.0625 to 0.0625
- up_weight: bfloat16 [16, 7168, 128], P('expert'), may hold values from -0.0625 to 0.0625
- down_weight: bfloat16 [16, 7168, 128], P('expert'), may hold values from -0.1875 to 0.1875
Outputs:
- mixed: bfloat16 [4096, 7168], P(('groups', 'expert')), parts along dimension 0
There are 2 independent parts, one for each index of `groups`. A program takes and returns all parts, laid end to end along the dimension named above; an argument that names none is the same for every part. Nothing has to cross between parts.
Inputs may be any that keep to these rules, and one draw needn't show every extreme that they name: `route_ids`: each row names 8 different experts. `capacity`: some slot accepts exactly 2. `placement`: expert ids are distinct and below 1; the old owner equals the expert id; new owners are distinct slots of 1 to 1.
All inputs are finite; a program needn't handle non-finite values.
Results may differ from a plain program's by a relative error of at most 0.0085.
Values may be sent and summed in bfloat16 or wider, within the bound.
No kernel may reach another device: no remote copies, remote signals or barrier semaphores. Data moves between devices by JAX's collectives and lax.ppermute only.
A program may use at most 64 MiB of HBM per device.

v0:
```python
import jax
import jax.numpy as jnp
from jax import lax
from jax.sharding import PartitionSpec as P

FF_W = 1024
HID_DEV = 128
CAP = 2


GATE_UNIT = 1.0 / 32768.0


def slot_tables(placement, slot_count):
    old_slot = placement[:, 0]
    new_slot = placement[:, 1]
    expert_id = placement[:, 2]
    slot_range = jnp.arange(slot_count, dtype=jnp.int32)
    is_named = expert_id[None, :] == slot_range[:, None]
    has_copy = jnp.any(is_named, axis=1)
    copy_slot = jnp.sum(jnp.where(is_named, new_slot[None, :], 0), axis=1)
    landing = new_slot[None, :] == slot_range[:, None]
    source_slot = jnp.where(
        jnp.any(landing, axis=1),
        jnp.sum(jnp.where(landing, old_slot[None, :], 0), axis=1),
        slot_range,
    )
    return (has_copy, copy_slot, source_slot)


def assign(route_ids, gate_fixed, capacity, has_copy, copy_slot, live_count, slot_rows):
    row_count = route_ids.shape[0]
    slot_count = capacity.shape[0]
    slot_range = jnp.arange(slot_count, dtype=jnp.int32)
    is_live = route_ids < live_count
    onehot = route_ids[:, :, None] == slot_range[None, None, :]
    doubled = jnp.any(onehot & has_copy[None, None, :], axis=2)
    copy_of = jnp.sum(jnp.where(onehot, copy_slot[None, None, :], 0), axis=2)
    odd_row = (jnp.arange(row_count, dtype=jnp.int32) % 2 == 1)[:, None]
    slot_of = jnp.where(doubled & odd_row, copy_of, jnp.where(is_live, route_ids, 0))
    flat_slot = slot_of.reshape(-1)
    flat_live = is_live.reshape(-1)
    member = ((flat_slot[:, None] == slot_range[None, :]) & flat_live[:, None]).astype(jnp.int32)
    before = jnp.cumsum(member, axis=0) - member
    position = jnp.sum(before * member, axis=1)
    allowed = jnp.sum(member * capacity[None, :], axis=1)
    kept_pair = flat_live & (position < allowed)
    target = flat_slot * slot_rows + position
    weight = jnp.where(kept_pair, gate_fixed.reshape(-1).astype(jnp.float32) * GATE_UNIT, 0.0)
    return (target, kept_pair, weight)


def tables(target, kept_pair, weight, row_count, table_width):
    column = jnp.arange(table_width, dtype=jnp.int32)
    matches = (target[:, None] == column[None, :]) & kept_pair[:, None]
    chosen = jnp.sum(matches.astype(jnp.int32).reshape(row_count, -1, table_width), axis=1)
    mixing = jnp.sum(
        (matches.astype(jnp.float32) * weight[:, None]).reshape(row_count, -1, table_width), axis=1
    )
    return (chosen, mixing)


def per_device(
    tokens, route_ids, gate_fixed, capacity, placement, gate_weight, up_weight, down_weight
):
    dev_count = lax.axis_size("expert")
    group_size = FF_W // HID_DEV
    slot_count = dev_count // group_size
    live_count = slot_count - placement.shape[0]
    row_count, model_width = tokens.shape
    has_copy, copy_slot, source_slot = slot_tables(placement, slot_count)
    target, kept_pair, weight = assign(
        route_ids, gate_fixed, capacity, has_copy, copy_slot, live_count, CAP
    )
    chosen, mixing = tables(target, kept_pair, weight, row_count, slot_count * CAP)
    slot_range = jnp.arange(slot_count, dtype=jnp.int32)
    owner_table = (source_slot[None, :] == slot_range[:, None]) & (
        source_slot[None, :] != slot_range[None, :]
    )
    gate_mat = gate_weight[0]
    up_mat = up_weight[0]
    down_mat = down_weight[0]
    picked = jnp.dot(
        chosen.T.astype(jnp.bfloat16), tokens, preferred_element_type=jnp.float32
    ).astype(jnp.bfloat16)
    slotted = picked.reshape(slot_count, CAP, model_width)
    block_rows = 2 * CAP
    extra = jnp.dot(
        owner_table.astype(jnp.bfloat16),
        slotted.reshape(slot_count, CAP * model_width),
        preferred_element_type=jnp.float32,
    )
    extra = extra.astype(jnp.bfloat16).reshape(slot_count, CAP, model_width)
    slotted = jnp.concatenate((slotted, extra), axis=1)
    outgoing = jnp.broadcast_to(
        slotted[:, None], (slot_count, group_size, block_rows, model_width)
    ).reshape(dev_count, block_rows, model_width)
    arrived = lax.all_to_all(outgoing, "expert", split_axis=0, concat_axis=0, tiled=True)
    flat_rows = arrived.reshape(-1, model_width)
    gate_val = jnp.dot(flat_rows, gate_mat, preferred_element_type=jnp.float32)
    up_val = jnp.dot(flat_rows, up_mat, preferred_element_type=jnp.float32)
    hidden = (jax.nn.silu(gate_val) * up_val).astype(jnp.bfloat16)
    partial_value = lax.dot_general(
        hidden, down_mat, (((1,), (1,)), ((), ())), preferred_element_type=jnp.float32
    )
    partial_value = partial_value.astype(jnp.bfloat16).reshape(
        arrived.shape[0], arrived.shape[1], model_width
    )
    returned = lax.all_to_all(partial_value, "expert", split_axis=0, concat_axis=0, tiled=True)
    summed = jnp.sum(
        returned.reshape(slot_count, group_size, block_rows, model_width), axis=1, dtype=jnp.float32
    )
    own_out = summed[:, :CAP]
    copy_out = summed[:, CAP:].reshape(slot_count, CAP * model_width)
    copy_back = jnp.dot(
        owner_table.T.astype(jnp.float32), copy_out, precision=lax.Precision.HIGHEST
    ).reshape(slot_count, CAP, model_width)
    is_landing = jnp.any(owner_table, axis=0)
    summed = jnp.where(is_landing[:, None, None], copy_back, own_out)
    combined = jnp.dot(
        mixing, summed.reshape(slot_count * CAP, model_width), precision=lax.Precision.HIGHEST
    )
    return combined.astype(jnp.bfloat16)


def solution(mesh):
    in_specs = (
        P(("groups", "expert"), None),
        P(("groups", "expert"), None),
        P(("groups", "expert"), None),
        P("groups"),
        P("groups", None),
        P("expert", None, None),
        P("expert", None, None),
        P("expert", None, None),
    )
    out_specs = P(("groups", "expert"), None)
    return jax.shard_map(
        per_device, mesh=mesh, in_specs=in_specs, out_specs=out_specs, check_vma=False
    )
```

profile of v0, /device:TPU:0, one launch (start us, length us, event | category | flops | bytes accessed | tf_op | source)
XLA Modules:
  0.0 83.3 jit_solution(13539430869862083441)
XLA Ops:
  0.0 1.5 %fusion.33 = (s32[1,1]{1,0:T(1,128)}, s32[1,1]{1,0:T(1,128)}, s32[1,1]{1,0:T(1,128)}) fusion(s32[1,3]{1,0:T(1,128)} %param.12), kind=kLoop, calls=%fused_computation.58 | loop fusion | bytes 24 | tf_op jit(solution)/shard_map/slice | solution.py:15
  1.5 0.7 iota_compare_fusion.4
  2.2 1.2 %broadcast_select_fusion = s32[2]{0:T(128)S(1)} fusion(s32[]{:T(128)} %bitcast.1, s32[]{:T(128)} %bitcast), kind=kLoop, calls=%fused_computation.54 | loop fusion | flops 4 | bytes 16 | tf_op jit(solution)/shard_map/jit(_where)/select_n | solution.py:21
  3.4 0.8 fusion.24
  4.2 0.8 select_reduce_fusion.2
  5.0 0.7 select_select_fusion
  6.3 0.6 reduce-window.6
  6.9 0.2 slice_reduce_fusion
  7.4 0.7 select_reduce_fusion.1
  8.4 0.7 multiply_select_fusion
  9.2 1.8 %convolution_convert_fusion.3 = bf16[4,7168]{1,0:T(4,128)(2,1)S(1)} fusion(bf16[128,7168]{1,0:T(8,128)(2,1)} %param.8, s32[128,4]{0,1:T(4,128)S(1)} %convert_reduce_fusion.1), kind=kOutput, calls=%fused_computation.4 | convolution fusion | flops 7369216 | bytes 1894400 | tf_op jit(solution)/shard_map/dot_general | solution.py:83
  11.1 1.2 %iota_compare_fusion.3 = (pred[2]{0:T(512)(128)(4,1)S(1)}, s32[2]{0:T(128)S(1)}) fusion(s32[]{:T(128)} %bitcast.3, s32[]{:T(128)} %bitcast.1), kind=kLoop, calls=%fused_computation.52 | loop fusion | flops 8 | bytes 18 | tf_op jit(solution)/shard_map/ne | solution.py:78
  12.3 0.3 convolution_convert_fusion
  12.8 0.2 broadcast_in_dim.84
  13.1 29.8 %all_to_all.10 = bf16[16,4,7168]{2,1,0:T(4,128)(2,1)} all-to-all(bf16[16,4,7168]{2,1,0:T(4,128)(2,1)S(1)} %bitcast.59), channel_id=1, replica_groups=mesh['groups'=2,'expert'=16] {'expert'}, dimensions={0} | all-to-all | bytes 1835008 | tf_op jit(solution)/shard_map/all_to_all | solution.py:98
  42.9 1.7 %reshape.183 = bf16[64,7168]{1,0:T(8,128)(2,1)S(1)} reshape(bf16[16,4,7168]{2,1,0:T(4,128)(2,1)} %all_to_all.10) | data formatting | bytes 1835008 | tf_op jit(solution)/shard_map/reshape | solution.py:99
  44.6 2.0 %fusion.3 = f32[64,128]{1,0:T(8,128)S(1)} fusion(bf16[64,7168]{1,0:T(8,128)(2,1)S(1)} %reshape.183, bf16[1,7168,128]{2,1,0:T(8,128)(2,1)} %param.13), kind=kOutput, calls=%fused_computation.9 | convolution fusion | flops 117440512 | bytes 2785280 | tf_op jit(solution)/shard_map/dot_general | solution.py:100
  46.6 3.6 %convolution_convert_fusion.2 = bf16[64,7168]{1,0:T(8,128)(2,1)} fusion(bf16[1,7168,128]{2,1,0:T(8,128)(2,1)S(1)} %copy-done, bf16[64,7168]{1,0:T(8,128)(2,1)S(1)} %reshape.183, bf16[1,7168,128]{2,1,0:T(8,128)(2,1)} %param.14, f32[64,128]{1,0:T(8,128)S(1)} %fusion.3), kind=kOutput, calls=%fused_computation.2 | convolution fusion | flops 235388928 | bytes 5537792 | tf_op jit(solution)/shard_map/dot_general | solution.py:103
  50.2 2.5 %reshape.184 = bf16[16,4,7168]{2,1,0:T(4,128)(2,1)} reshape(bf16[64,7168]{1,0:T(8,128)(2,1)} %convolution_convert_fusion.2) | data formatting | bytes 1835008 | tf_op jit(solution)/shard_map/reshape | solution.py:106
  52.7 4.5 %all-to-all-start.1 = ((bf16[16,4,7168]{2,1,0:T(4,128)(2,1)}), bf16[16,4,7168]{2,1,0:T(4,128)(2,1)S(1)}, u32[]{:S(2)}, u32[]{:S(2)}) async-start(bf16[16,4,7168]{2,1,0:T(4,128)(2,1)} %reshape.184), calls=%async_computation.1 | async-start | bytes 1835008 | tf_op jit(solution)/shard_map/all_to_all | solution.py:109
  57.4 20.6 %all-to-all-done.1 = bf16[16,4,7168]{2,1,0:T(4,128)(2,1)S(1)} async-done(((bf16[16,4,7168]{2,1,0:T(4,128)(2,1)}), bf16[16,4,7168]{2,1,0:T(4,128)(2,1)S(1)}, u32[]{:S(2)}, u32[]{:S(2)}) %all-to-all-start.1) | async-done | bytes 917536 | tf_op jit(solution)/shard_map/all_to_all | solution.py:109
  78.0 0.4 convert_reduce_fusion
  78.5 0.4 convolution_select_fusion
  79.1 4.3 %convolution_convert_fusion.1 = bf16[128,7168]{1,0:T(8,128)(2,1)} fusion(f32[128,4]{0,1:T(4,128)S(1)} %select_reduce_fusion, f32[4,7168]{1,0:T(4,128)S(1)} %reshape.186), kind=kOutput, calls=%fused_computation.1 | convolution fusion | flops 44957696 | bytes 1951744 | tf_op jit(solution)/shard_map/dot_general | solution.py:120
  (27 shorter events, 1.9 us)
Async XLA Ops:
  0.0 46.5 %copy-start = (bf16[1,7168,128]{2,1,0:T(8,128)(2,1)S(1)}, bf16[1,7168,128]{2,1,0:T(8,128)(2,1)}, u32[]{:S(2)}) copy-start(bf16[1,7168,128]{2,1,0:T(8,128)(2,1)} %param.15) | copy-start | bytes 5505028
  52.7 25.3 %all-to-all-start.1 = ((bf16[16,4,7168]{2,1,0:T(4,128)(2,1)}), bf16[16,4,7168]{2,1,0:T(4,128)(2,1)S(1)}, u32[]{:S(2)}, u32[]{:S(2)}) async-start(bf16[16,4,7168]{2,1,0:T(4,128)(2,1)} %reshape.184), calls=%async_computation.1 | async-start | bytes 1835008 | tf_op jit(solution)/shard_map/all_to_all | solution.py:109
where the time goes:
time: 84.5 us; the launch traced here: 83.3 us
  blocking collectives  29.8 us (35%)
  waiting for transfers between devices  20.6 us (24%)
  matrix products  12.4 us (15%)
  other arithmetic  8.44 us (10%)
  local copies, waits for them, and re-layouts  7.38 us (9%)
  starting transfers between devices  4.48 us (5%)
    all_to_all x1, blocking collectives, per_device(): lax.all_to_all(outgoing, 'expert', split_axis=0, concat_axis=0, tiled=True)  29.8 us
    all_to_all x1, waiting for transfers between devices, per_device(): lax.all_to_all(partial_value, 'expert', split_axis=0, concat_axis=0, tile...  20.6 us
    all_to_all x1, starting transfers between devices, per_device(): lax.all_to_all(partial_value, 'expert', split_axis=0, concat_axis=0, tile...  4.48 us
    dot_general x1, matrix products, per_device(): jnp.dot(mixing, summed.reshape(slot_count * CAP, model_width), precision=...  4.25 us
    dot_general x1, matrix products, per_device(): lax.dot_general(hidden, down_mat, (((1,), (1,)), ((), ())), preferred_ele...  3.59 us
    reshape x1, local copies, waits for them, and re-layouts, per_device(): partial_value.astype(jnp.bfloat16)  2.52 us
    dot_general x1, matrix products, per_device(): gate_val = jnp.dot(flat_rows, gate_mat, preferred_element_type=jnp.float32)  1.96 us
    dot_general x1, matrix products, per_device(): jnp.dot(chosen.T.astype(jnp.bfloat16), tokens, preferred_element_type=jnp...  1.85 us
  transfers between devices with their start and end apart: 1, of which 1 were waited for; matrix products, arithmetic and copies ran while one was open for 0% of the time, Pallas kernels for 0%

commit v1 on v0

--- a/solution.py
+++ b/solution.py
@@ -1,6 +1,8 @@
 import jax
 import jax.numpy as jnp
 from jax import lax
+from jax.experimental import pallas as pl
+from jax.experimental.pallas import tpu as pltpu
 from jax.sharding import PartitionSpec as P
 
 FF_W = 1024
@@ -60,7 +62,7 @@
     return (chosen, mixing)
 
 
-def per_device(
+def per_device_general(
     tokens, route_ids, gate_fixed, capacity, placement, gate_weight, up_weight, down_weight
 ):
     dev_count = lax.axis_size("expert")
@@ -122,6 +124,179 @@
     )
     return combined.astype(jnp.bfloat16)
 
+MIB = 1024 * 1024
+
+
+def route_kernel(route_ref, gate_ref, cap_ref, tokens_ref, picked_ref, mix_ref, held, sem):
+    row_count = held.shape[0]
+    fetch = pltpu.make_async_copy(tokens_ref, held, sem)
+    fetch.start()
+    hit = route_ref[...] == 0
+    member = jnp.sum(jnp.where(hit, 1.0, 0.0), axis=1, keepdims=True)
+    fixed = jnp.sum(jnp.where(hit, gate_ref[...], 0), axis=1, keepdims=True)
+    shape = (row_count, 128)
+    weight = jnp.broadcast_to(fixed.astype(jnp.float32) * GATE_UNIT, shape)
+    member = jnp.broadcast_to(member, shape)
+    row = lax.broadcasted_iota(jnp.int32, (row_count, row_count), 0)
+    col = lax.broadcasted_iota(jnp.int32, (row_count, row_count), 1)
+    earlier = jnp.where((col < row) & (((row - col) & 1) == 0), 1.0, 0.0).astype(jnp.bfloat16)
+    before = jnp.dot(earlier, member.astype(jnp.bfloat16), preferred_element_type=jnp.float32)
+    token = lax.broadcasted_iota(jnp.int32, shape, 0)
+    odd = (token & 1) == 1
+    limit = jnp.where(odd, cap_ref[1], cap_ref[0]).astype(jnp.float32)
+    kept = (member > 0.5) & (before < limit)
+    spots = []
+    for place in range(CAP):
+        here = kept & (before == float(place))
+        mix_ref[place] = jnp.where(here, weight, 0.0)
+        for slot in range(2):
+            mine = here & (odd if slot == 1 else jnp.logical_not(odd))
+            spots.append(jnp.max(jnp.where(mine, token, -1), axis=0, keepdims=True))
+    spots = [spots[place * 2 + slot][0, 0] for slot in range(2) for place in range(CAP)]
+    fetch.wait()
+    lines = lax.broadcasted_iota(jnp.int32, (16, 1), 0)
+    rows = []
+    for spot in spots:
+        base = pl.multiple_of((jnp.maximum(spot, 0) // 16) * 16, 16)
+        block = held[pl.ds(base, 16), :].astype(jnp.float32)
+        rows.append(jnp.sum(jnp.where(lines == spot - base, block, 0.0), axis=0, keepdims=True))
+    picked_ref[...] = jnp.concatenate(rows, axis=0).astype(jnp.bfloat16)
+
+
+def expert_kernel(*refs):
+    pieces = refs[:8]
+    gate_a, gate_b, up_a, up_b, down_a, down_b = refs[8:14]
+    outs = refs[14:22]
+    rows_ref = refs[22]
+    width = rows_ref.shape[1]
+    for pair in range(4):
+        both = jnp.concatenate(
+            [pieces[2 * pair][...].astype(jnp.float32), pieces[2 * pair + 1][...].astype(jnp.float32)], axis=0
+        )
+        rows_ref[pl.ds(8 * pair, 8), :] = both
+    step = 256
+    acc_a = jnp.zeros((32, 2 * HID_DEV), jnp.float32)
+    acc_b = jnp.zeros((32, 2 * HID_DEV), jnp.float32)
+    for start in range(0, width, step):
+        part = pl.ds(start, step)
+        left = rows_ref[:, part].astype(jnp.bfloat16)
+        wa = jnp.concatenate([gate_a[part, :], up_a[part, :]], axis=1)
+        wb = jnp.concatenate([gate_b[part, :], up_b[part, :]], axis=1)
+        acc_a = acc_a + jnp.dot(left, wa, preferred_element_type=jnp.float32)
+        acc_b = acc_b + jnp.dot(left, wb, preferred_element_type=jnp.float32)
+    hidden = []
+    for acc in (acc_a, acc_b):
+        gate_val = acc[:, :HID_DEV]
+        up_val = acc[:, HID_DEV:]
+        hidden.append((gate_val / (1.0 + jnp.exp(-gate_val)) * up_val).astype(jnp.bfloat16))
+    hidden = jnp.concatenate(hidden, axis=1)
+    for start in range(0, width, step):
+        part = pl.ds(start, step)
+        down = jnp.concatenate([down_a[part, :], down_b[part, :]], axis=1)
+        value = lax.dot_general(
+            hidden, down, (((1,), (1,)), ((), ())), preferred_element_type=jnp.float32
+        )
+        for index in range(8):
+            outs[index][:, part] = value[4 * index : 4 * index + 4].astype(jnp.bfloat16)
+
+
+def combine_kernel(serves_ref, own, from_2, from_4, from_6, folded, mix_ref, out_ref, built, sems):
+    serves = serves_ref[0] > 0
+    total = own[...].astype(jnp.float32)
+    for ref in (from_2, from_4, from_6):
+        total = total + ref[...].astype(jnp.float32)
+    total = jnp.where(serves, total, folded[...].astype(jnp.float32))
+    width = total.shape[1]
+    odd = (lax.broadcasted_iota(jnp.int32, (16, 1), 0) & 1) == 1
+    lanes = [
+        jnp.where(odd, total[CAP + place : CAP + place + 1], total[place : place + 1])
+        for place in range(CAP)
+    ]
+    copies = []
+    for block in range(out_ref.shape[0] // 16):
+        part = pl.ds(16 * block, 16)
+        value = mix_ref[0, part, :1] * lanes[0] + mix_ref[1, part, :1] * lanes[1]
+        built[part, :] = value.astype(jnp.bfloat16)
+        copies.append(pltpu.make_async_copy(built.at[part], out_ref.at[part], sems.at[block]))
+        copies[-1].start()
+    for copy in copies:
+        copy.wait()
+
+
+def per_device_pair(
+    tokens, route_ids, gate_fixed, capacity, placement, gate_weight, up_weight, down_weight
+):
+    dev_count = lax.axis_size("expert")
+    row_count, model_width = tokens.shape
+    vmem = pl.BlockSpec(memory_space=pltpu.VMEM)
+    smem = pl.BlockSpec(memory_space=pltpu.SMEM)
+    anywhere = pl.BlockSpec(memory_space=pl.ANY)
+
+    def swap(value, offset):
+        return lax.ppermute(value, "expert", [(i, i ^ offset) for i in range(dev_count)])
+
+    picked, mix = pl.pallas_call(
+        route_kernel,
+        out_shape=(
+            jax.ShapeDtypeStruct((2 * CAP, model_width), jnp.bfloat16),
+            jax.ShapeDtypeStruct((CAP, row_count, 128), jnp.float32),
+        ),
+        in_specs=[vmem, vmem, smem, anywhere],
+        out_specs=(vmem, vmem),
+        scratch_shapes=[
+            pltpu.VMEM((row_count, model_width), jnp.bfloat16),
+            pltpu.SemaphoreType.DMA,
+        ],
+        compiler_params=pltpu.CompilerParams(vmem_limit_bytes=16 * MIB),
+        name="route",
+    )(route_ids, gate_fixed, capacity, tokens)
+    gate_a, up_a, down_a = gate_weight[0], up_weight[0], down_weight[0]
+    gate_b, up_b, down_b = (swap(value, 1) for value in (gate_a, up_a, down_a))
+    fold = swap(picked, 8)
+    own_pieces = [picked] + [swap(picked, k) for k in (2, 4, 6)]
+    fold_pieces = [fold] + [swap(fold, k) for k in (2, 4, 6)]
+    piece = jax.ShapeDtypeStruct((2 * CAP, model_width), jnp.bfloat16)
+    outs = pl.pallas_call(
+        expert_kernel,
+        out_shape=(piece,) * 8,
+        in_specs=[vmem] * 14,
+        out_specs=(vmem,) * 8,
+        scratch_shapes=[pltpu.VMEM((32, model_width), jnp.float32)],
+        compiler_params=pltpu.CompilerParams(vmem_limit_bytes=24 * MIB),
+        name="experts",
+    )(*own_pieces, *fold_pieces, gate_a, gate_b, up_a, up_b, down_a, down_b)
+    own_out, fold_out = outs[:4], outs[4:]
+    fold_back = [swap(fold_out[i], k) for i, k in ((1, 2), (2, 4), (3, 6))]
+    own_back = [swap(own_out[i], k) for i, k in ((1, 2), (2, 4), (3, 6))]
+    fold_sum = fold_out[0].astype(jnp.float32)
+    for value in fold_back:
+        fold_sum = fold_sum + value.astype(jnp.float32)
+    returned = swap(fold_sum.astype(jnp.bfloat16), 8)
+    serves = (lax.axis_index("expert") < dev_count // 2).astype(jnp.int32).reshape(1)
+    return pl.pallas_call(
+        combine_kernel,
+        out_shape=jax.ShapeDtypeStruct((row_count, model_width), jnp.bfloat16),
+        in_specs=[smem] + [vmem] * 6,
+        out_specs=anywhere,
+        scratch_shapes=[
+            pltpu.VMEM((row_count, model_width), jnp.bfloat16),
+            pltpu.SemaphoreType.DMA((row_count // 16,)),
+        ],
+        compiler_params=pltpu.CompilerParams(vmem_limit_bytes=16 * MIB),
+        name="combine",
+    )(serves, own_out[0], *own_back, returned, mix)
+
+
+def per_device(
+    tokens, route_ids, gate_fixed, capacity, placement, gate_weight, up_weight, down_weight
+):
+    group_size = FF_W // HID_DEV
+    pair = lax.axis_size("expert") == 2 * group_size and placement.shape[0] == 1 and group_size == 8
+    step = per_device_pair if pair else per_device_general
+    return step(
+        tokens, route_ids, gate_fixed, capacity, placement, gate_weight, up_weight, down_weight
+    )
+
 
 def solution(mesh):
     in_specs = (

time: 84.5 us -> 50.4 us (0.60); the launches traced: 83.3 us -> 50.2 us
  blocking collectives: 29.8 us -> 0 us
  starting transfers between devices: 4.48 us -> 23.6 us
  matrix products: 12.4 us -> 0 us
  other arithmetic: 8.44 us -> 0.06 us
  waiting for transfers between devices: 20.6 us -> 12.4 us
  Pallas kernels: 0 us -> 7.37 us
    all_to_all x1 -> x0, blocking collectives: 29.8 us -> none  [per_device(): lax.all_to_all(outgoing, 'expert', split_axis=0, concat_axis=0, tiled=True)]
    ppermute x0 -> x17, starting transfers between devices: none -> 23.6 us  [swap(): lax.ppermute(value, 'expert', [(i, i ^ offset) for i in range(dev_count)])]
    all_to_all x1 -> x0, waiting for transfers between devices: 20.6 us -> none  [per_device(): lax.all_to_all(partial_value, 'expert', split_axis=0, concat_axis=0, tile...]
    dot_general x6 -> x0, matrix products: 12.4 us -> none  [the longest x1 4.25 us: per_device(): jnp.dot(mixing, summed.reshape(slot_count * CAP, model_width), precision=...]
    ppermute x0 -> x17, waiting for transfers between devices: none -> 12.4 us  [swap(): lax.ppermute(value, 'expert', [(i, i ^ offset) for i in range(dev_count)])]
    pallas_call x0 -> x3, Pallas kernels: none -> 7.37 us  [the longest x1 4.35 us: per_device_pair(): pl.pallas_call(expert_kernel, out_shape=(piece,) * 8, in_specs=[vmem] * 1...]
    unnamed x2 -> x12, local copies, waits for them, and re-layouts: 0.01 us -> 6.72 us
    all_to_all x1 -> x0, starting transfers between devices: 4.48 us -> none  [per_device(): lax.all_to_all(partial_value, 'expert', split_axis=0, concat_axis=0, tile...]
  transfers between devices with their start and end apart: 1 -> 17, of which waited for: 1 -> 8; matrix products, arithmetic and copies ran while one was open for 0% -> 3% of each run, Pallas kernels for 0% -> 3%
where the time goes in v1:
time: 50.4 us; the launch traced here: 50.2 us
  starting transfers between devices  23.6 us (47%)
  waiting for transfers between devices  12.4 us (25%)
  Pallas kernels  7.37 us (15%)
  local copies, waits for them, and re-layouts  6.72 us (13%)
    ppermute x17, starting transfers between devices, swap(): lax.ppermute(value, 'expert', [(i, i ^ offset) for i in range(dev_count)])  23.6 us
    ppermute x17, waiting for transfers between devices, swap(): lax.ppermute(value, 'expert', [(i, i ^ offset) for i in range(dev_count)])  12.4 us
    unnamed x12, local copies, waits for them, and re-layouts  6.72 us
    pallas_call x1, Pallas kernels, per_device_pair(): pl.pallas_call(expert_kernel, out_shape=(piece,) * 8, in_specs=[vmem] * 1...  4.35 us
    pallas_call x1, Pallas kernels, per_device_pair(): pl.pallas_call(combine_kernel, out_shape=jax.ShapeDtypeStruct((row_count,...  1.68 us
    pallas_call x1, Pallas kernels, per_device_pair(): pl.pallas_call(route_kernel, out_shape=(jax.ShapeDtypeStruct((2 * CAP, mo...  1.34 us
  transfers between devices with their start and end apart: 17, of which 8 were waited for; matrix products, arithmetic and copies ran while one was open for 3% of the time, Pallas kernels for 3%

profile of v1, /device:TPU:0, one launch (start us, length us, event | category | flops | bytes accessed | tf_op | source)
XLA Modules:
  0.0 50.2 jit_solution(12933259115321463139)
XLA Ops:
  2.5 1.5 %copy-done = bf16[128,7168]{1,0:T(8,128)(2,1)S(1)} copy-done((bf16[128,7168]{1,0:T(8,128)(2,1)S(1)}, bf16[128,7168]{1,0:T(8,128)(2,1)}, u32[]{:S(2)}) %copy-start) | copy-done | bytes 1835032
  4.7 1.3 %route.1 = (bf16[4,7168]{1,0:T(4,128)(2,1)S(1)}, f32[2,128,128]{2,1,0:T(8,128)S(1)}) custom-call(s32[128,8]{1,0:T(8,128)S(1)} %copy.8.route_ref, s32[128,8]{1,0:T(8,128)S(1)} %copy.9.gate_ref, s32[2]{0:T(128)S(1)} %copy-done.4, bf16[128,7168]{1,0:T(8,128)(2,1)S(1)} %copy-done), custom_call_target="tpu_custom_call" | custom-call | tf_op jit(solution)/shard_map/route/pallas_call | solution.py:238
  6.0 3.7 %collective-permute-start.3 = (bf16[4,7168]{1,0:T(4,128)(2,1)S(1)}, bf16[4,7168]{1,0:T(4,128)(2,1)S(1)}, u32[]{:S(2)}, u32[]{:S(2)}) collective-permute-start(bf16[4,7168]{1,0:T(4,128)(2,1)S(1)} %get-tuple-element.15.refs_0_), channel_id=1, source_target_pairs={{0,8},{1,9},{2,10},{3,11},{4,12},{5,13},{6,14},{7,15},{8,0},{9,1},... | collective-permute-start | bytes 172040 | tf_op jit(solution)/shard_map/ppermute | solution.py:236
  9.7 1.5 %collective-permute-start = (bf16[4,7168]{1,0:T(4,128)(2,1)S(1)}, bf16[4,7168]{1,0:T(4,128)(2,1)S(1)}, u32[]{:S(2)}, u32[]{:S(2)}) collective-permute-start(bf16[4,7168]{1,0:T(4,128)(2,1)S(1)} %get-tuple-element.15.refs_0_), channel_id=1, source_target_pairs={{0,2},{1,3},{2,0},{3,1},{4,6},{5,7},{6,4},{7,5},{8,10},{9,11},{10,... | collective-permute-start | bytes 172040 | tf_op jit(solution)/shard_map/ppermute | solution.py:236
  11.2 2.3 %collective-permute-done.3.refs_4_ = bf16[4,7168]{1,0:T(4,128)(2,1)S(1)} collective-permute-done((bf16[4,7168]{1,0:T(4,128)(2,1)S(1)}, bf16[4,7168]{1,0:T(4,128)(2,1)S(1)}, u32[]{:S(2)}, u32[]{:S(2)}) %collective-permute-start.3) | collective-permute-done | bytes 57376 | tf_op jit(solution)/shard_map/ppermute | solution.py:236
  14.3 2.3 %collective-permute-start.2 = (bf16[4,7168]{1,0:T(4,128)(2,1)S(1)}, bf16[4,7168]{1,0:T(4,128)(2,1)S(1)}, u32[]{:S(2)}, u32[]{:S(2)}) collective-permute-start(bf16[4,7168]{1,0:T(4,128)(2,1)S(1)} %get-tuple-element.15.refs_0_), channel_id=1, source_target_pairs={{0,6},{1,7},{2,4},{3,5},{4,2},{5,3},{6,0},{7,1},{8,14},{9,15},{10,... | collective-permute-start | bytes 172040 | tf_op jit(solution)/shard_map/ppermute | solution.py:236
  16.5 1.3 %collective-permute-done.1.refs_2_ = bf16[4,7168]{1,0:T(4,128)(2,1)S(1)} collective-permute-done((bf16[4,7168]{1,0:T(4,128)(2,1)S(1)}, bf16[4,7168]{1,0:T(4,128)(2,1)S(1)}, u32[]{:S(2)}, u32[]{:S(2)}) %collective-permute-start.1) | collective-permute-done | bytes 57376 | tf_op jit(solution)/shard_map/ppermute | solution.py:236
  17.9 1.4 %collective-permute-start.4 = (bf16[4,7168]{1,0:T(4,128)(2,1)S(1)}, bf16[4,7168]{1,0:T(4,128)(2,1)S(1)}, u32[]{:S(2)}, u32[]{:S(2)}) collective-permute-start(bf16[4,7168]{1,0:T(4,128)(2,1)S(1)} %collective-permute-done.3.refs_4_), channel_id=1, source_target_pairs={{0,2},{1,3},{2,0},{3,1},{4,6},{5,7},{6,4},{7,5},{8,10},{9,11},{10,... | collective-permute-start | bytes 172040 | tf_op jit(solution)/shard_map/ppermute | solution.py:236
  19.5 1.3 %collective-permute-start.5 = (bf16[4,7168]{1,0:T(4,128)(2,1)S(1)}, bf16[4,7168]{1,0:T(4,128)(2,1)S(1)}, u32[]{:S(2)}, u32[]{:S(2)}) collective-permute-start(bf16[4,7168]{1,0:T(4,128)(2,1)S(1)} %collective-permute-done.3.refs_4_), channel_id=1, source_target_pairs={{0,4},{1,5},{2,6},{3,7},{4,0},{5,1},{6,2},{7,3},{8,12},{9,13},{10,... | collective-permute-start | bytes 172040 | tf_op jit(solution)/shard_map/ppermute | solution.py:236
  20.7 1.3 %collective-permute-done.4.refs_5_ = bf16[4,7168]{1,0:T(4,128)(2,1)S(1)} collective-permute-done((bf16[4,7168]{1,0:T(4,128)(2,1)S(1)}, bf16[4,7168]{1,0:T(4,128)(2,1)S(1)}, u32[]{:S(2)}, u32[]{:S(2)}) %collective-permute-start.4) | collective-permute-done | bytes 57376 | tf_op jit(solution)/shard_map/ppermute | solution.py:236
  22.0 1.8 %collective-permute-start.6 = (bf16[4,7168]{1,0:T(4,128)(2,1)S(1)}, bf16[4,7168]{1,0:T(4,128)(2,1)S(1)}, u32[]{:S(2)}, u32[]{:S(2)}) collective-permute-start(bf16[4,7168]{1,0:T(4,128)(2,1)S(1)} %collective-permute-done.3.refs_4_), channel_id=1, source_target_pairs={{0,6},{1,7},{2,4},{3,5},{4,2},{5,3},{6,0},{7,1},{8,14},{9,15},{10,... | collective-permute-start | bytes 172040 | tf_op jit(solution)/shard_map/ppermute | solution.py:236
  24.2 2.9 %collective-permute-done.6.refs_7_ = bf16[4,7168]{1,0:T(4,128)(2,1)S(1)} collective-permute-done((bf16[4,7168]{1,0:T(4,128)(2,1)S(1)}, bf16[4,7168]{1,0:T(4,128)(2,1)S(1)}, u32[]{:S(2)}, u32[]{:S(2)}) %collective-permute-start.6) | collective-permute-done | bytes 57376 | tf_op jit(solution)/shard_map/ppermute | solution.py:236
  27.2 1.5 %copy-done.2 = bf16[1,7168,128]{2,1,0:T(8,128)(2,1)S(1)} copy-done((bf16[1,7168,128]{2,1,0:T(8,128)(2,1)S(1)}, bf16[1,7168,128]{2,1,0:T(8,128)(2,1)}, u32[]{:S(2)}) %copy-start.2) | copy-done | bytes 1835032
  28.7 1.5 %copy-done.3 = bf16[1,7168,128]{2,1,0:T(8,128)(2,1)S(1)} copy-done((bf16[1,7168,128]{2,1,0:T(8,128)(2,1)S(1)}, bf16[1,7168,128]{2,1,0:T(8,128)(2,1)}, u32[]{:S(2)}) %copy-start.3) | copy-done | bytes 1835032
  30.2 4.3 %experts.1 = (bf16[4,7168]{1,0:T(4,128)(2,1)S(1)}, bf16[4,7168]{1,0:T(4,128)(2,1)S(1)}, bf16[4,7168]{1,0:T(4,128)(2,1)S(1)}, bf16[4,7168]{1,0:T(4,128)(2,1)S(1)}...) custom-call(bf16[4,7168]{1,0:T(4,128)(2,1)S(1)} %get-tuple-element.1, ...), custom_call_target="tpu_custom_call" | custom-call | tf_op jit(solution)/shard_map/experts/pallas_call | solution.py:259
  34.5 1.5 %collective-permute-start.13 = (bf16[4,7168]{1,0:T(4,128)(2,1)S(1)}, bf16[4,7168]{1,0:T(4,128)(2,1)S(1)}, u32[]{:S(2)}, u32[]{:S(2)}) collective-permute-start(bf16[4,7168]{1,0:T(4,128)(2,1)S(1)} %get-tuple-element.21), channel_id=1, source_target_pairs={{0,2},{1,3},{2,0},{3,1},{4,6},{5,7},{6,4},{7,5},{8,10},{9,11},{10,... | collective-permute-start | bytes 172040 | tf_op jit(solution)/shard_map/ppermute | solution.py:236
  36.0 1.0 %collective-permute-start.14 = (bf16[4,7168]{1,0:T(4,128)(2,1)S(1)}, bf16[4,7168]{1,0:T(4,128)(2,1)S(1)}, u32[]{:S(2)}, u32[]{:S(2)}) collective-permute-start(bf16[4,7168]{1,0:T(4,128)(2,1)S(1)} %get-tuple-element.22), channel_id=1, source_target_pairs={{0,4},{1,5},{2,6},{3,7},{4,0},{5,1},{6,2},{7,3},{8,12},{9,13},{10,... | collective-permute-start | bytes 172040 | tf_op jit(solution)/shard_map/ppermute | solution.py:236
  37.0 1.1 %collective-permute-start.15 = (bf16[4,7168]{1,0:T(4,128)(2,1)S(1)}, bf16[4,7168]{1,0:T(4,128)(2,1)S(1)}, u32[]{:S(2)}, u32[]{:S(2)}) collective-permute-start(bf16[4,7168]{1,0:T(4,128)(2,1)S(1)} %get-tuple-element.23), channel_id=1, source_target_pairs={{0,6},{1,7},{2,4},{3,5},{4,2},{5,3},{6,0},{7,1},{8,14},{9,15},{10,... | collective-permute-start | bytes 172040 | tf_op jit(solution)/shard_map/ppermute | solution.py:236
  38.1 1.4 %collective-permute-start.10 = (bf16[4,7168]{1,0:T(4,128)(2,1)S(1)}, bf16[4,7168]{1,0:T(4,128)(2,1)S(1)}, u32[]{:S(2)}, u32[]{:S(2)}) collective-permute-start(bf16[4,7168]{1,0:T(4,128)(2,1)S(1)} %get-tuple-element.17), channel_id=1, source_target_pairs={{0,2},{1,3},{2,0},{3,1},{4,6},{5,7},{6,4},{7,5},{8,10},{9,11},{10,... | collective-permute-start | bytes 172040 | tf_op jit(solution)/shard_map/ppermute | solution.py:236
  40.5 1.1 %collective-permute-start.12 = (bf16[4,7168]{1,0:T(4,128)(2,1)S(1)}, bf16[4,7168]{1,0:T(4,128)(2,1)S(1)}, u32[]{:S(2)}, u32[]{:S(2)}) collective-permute-start(bf16[4,7168]{1,0:T(4,128)(2,1)S(1)} %get-tuple-element.19), channel_id=1, source_target_pairs={{0,6},{1,7},{2,4},{3,5},{4,2},{5,3},{6,0},{7,1},{8,14},{9,15},{10,... | collective-permute-start | bytes 172040 | tf_op jit(solution)/shard_map/ppermute | solution.py:236
  41.6 1.1 %collective-permute-done.15 = bf16[4,7168]{1,0:T(4,128)(2,1)S(1)} collective-permute-done((bf16[4,7168]{1,0:T(4,128)(2,1)S(1)}, bf16[4,7168]{1,0:T(4,128)(2,1)S(1)}, u32[]{:S(2)}, u32[]{:S(2)}) %collective-permute-start.15) | collective-permute-done | bytes 57376 | tf_op jit(solution)/shard_map/ppermute | solution.py:236
  42.7 2.8 %collective-permute-start.16 = (bf16[4,7168]{1,0:T(4,128)(2,1)S(1)}, bf16[4,7168]{1,0:T(4,128)(2,1)S(1)}, u32[]{:S(2)}, u32[]{:S(2)}) collective-permute-start(bf16[4,7168]{1,0:T(4,128)(2,1)S(1)} %add_convert_fusion), channel_id=1, source_target_pairs={{0,8},{1,9},{2,10},{3,11},{4,12},{5,13},{6,14},{7,15},{8,0},{9,1},... | collective-permute-start | bytes 172040 | tf_op jit(solution)/shard_map/ppermute | solution.py:236
  45.6 2.9 %collective-permute-done.16.folded = bf16[4,7168]{1,0:T(4,128)(2,1)S(1)} collective-permute-done((bf16[4,7168]{1,0:T(4,128)(2,1)S(1)}, bf16[4,7168]{1,0:T(4,128)(2,1)S(1)}, u32[]{:S(2)}, u32[]{:S(2)}) %collective-permute-start.16) | collective-permute-done | bytes 57376 | tf_op jit(solution)/shard_map/ppermute | solution.py:236
  48.5 1.7 %combine.1 = bf16[128,7168]{1,0:T(8,128)(2,1)} custom-call(s32[1]{0:T(128)} %bitcast.serves_ref, bf16[4,7168]{1,0:T(4,128)(2,1)S(1)} %get-tuple-element.16.own, bf16[4,7168]{1,0:T(4,128)(2,1)S(1)} %collective-permute-done.10.from_2, bf16[4,7168]{1,0:T(4,128)(2,1)S(1)} %collective-permute-done.11.from_4, bf16[4,7168]{1,0:T(4,128)(2,1)S(1)} %collective-permute-done.12.from_6, ...), custom_call_target="tpu_custom_call" | custom-call | tf_op jit(solution)/shard_map/combine/pallas_call | solution.py:276
  (26 shorter events, 5.5 us)
Async XLA Ops:
  0.0 27.1 %collective-permute-start.7 = (bf16[7168,128]{1,0:T(8,128)(2,1)}, bf16[7168,128]{1,0:T(8,128)(2,1)S(1)}, u32[]{:S(2)}, u32[]{:S(2)}) collective-permute-start(bf16[7168,128]{1,0:T(8,128)(2,1)} %bitcast.4), channel_id=1, source_target_pairs={{0,1},{1,0},{2,3},{3,2},{4,5},{5,4},{6,7},{7,6},{8,9},{9,8},{10,11... | collective-permute-start | bytes 5505032 | tf_op jit(solution)/shard_map/ppermute | solution.py:236
  0.5 26.7 %collective-permute-start.8 = (bf16[7168,128]{1,0:T(8,128)(2,1)}, bf16[7168,128]{1,0:T(8,128)(2,1)}, u32[]{:S(2)}, u32[]{:S(2)}) collective-permute-start(bf16[7168,128]{1,0:T(8,128)(2,1)} %bitcast.6), channel_id=1, source_target_pairs={{0,1},{1,0},{2,3},{3,2},{4,5},{5,4},{6,7},{7,6},{8,9},{9,8},{10,11... | collective-permute-start | bytes 5505032 | tf_op jit(solution)/shard_map/ppermute | solution.py:236
  0.5 26.6 %collective-permute-start.9 = (bf16[7168,128]{1,0:T(8,128)(2,1)}, bf16[7168,128]{1,0:T(8,128)(2,1)}, u32[]{:S(2)}, u32[]{:S(2)}) collective-permute-start(bf16[7168,128]{1,0:T(8,128)(2,1)} %bitcast.8), channel_id=1, source_target_pairs={{0,1},{1,0},{2,3},{3,2},{4,5},{5,4},{6,7},{7,6},{8,9},{9,8},{10,11... | collective-permute-start | bytes 5505032 | tf_op jit(solution)/shard_map/ppermute | solution.py:236
  2.5 1.5 %copy-start = (bf16[128,7168]{1,0:T(8,128)(2,1)S(1)}, bf16[128,7168]{1,0:T(8,128)(2,1)}, u32[]{:S(2)}) copy-start(bf16[128,7168]{1,0:T(8,128)(2,1)} %tokens_ref.1) | copy-start | bytes 5505028
  4.0 0.7 %copy-start.4 = (s32[2]{0:T(128)S(1)}, s32[2]{0:T(128)}, u32[]{:S(2)}) copy-start(s32[2]{0:T(128)} %cap_ref.1) | copy-start | bytes 28
  4.7 22.4 %copy-start.1 = (bf16[1,7168,128]{2,1,0:T(8,128)(2,1)S(1)}, bf16[1,7168,128]{2,1,0:T(8,128)(2,1)}, u32[]{:S(2)}) copy-start(bf16[1,7168,128]{2,1,0:T(8,128)(2,1)} %param.12) | copy-start | bytes 5505028
  6.0 7.5 %collective-permute-start.3 = (bf16[4,7168]{1,0:T(4,128)(2,1)S(1)}, bf16[4,7168]{1,0:T(4,128)(2,1)S(1)}, u32[]{:S(2)}, u32[]{:S(2)}) collective-permute-start(bf16[4,7168]{1,0:T(4,128)(2,1)S(1)} %get-tuple-element.15.refs_0_), channel_id=1, source_target_pairs={{0,8},{1,9},{2,10},{3,11},{4,12},{5,13},{6,14},{7,15},{8,0},{9,1},... | collective-permute-start | bytes 172040 | tf_op jit(solution)/shard_map/ppermute | solution.py:236
  9.7 4.6 %collective-permute-start = (bf16[4,7168]{1,0:T(4,128)(2,1)S(1)}, bf16[4,7168]{1,0:T(4,128)(2,1)S(1)}, u32[]{:S(2)}, u32[]{:S(2)}) collective-permute-start(bf16[4,7168]{1,0:T(4,128)(2,1)S(1)} %get-tuple-element.15.refs_0_), channel_id=1, source_target_pairs={{0,2},{1,3},{2,0},{3,1},{4,6},{5,7},{6,4},{7,5},{8,10},{9,11},{10,... | collective-permute-start | bytes 172040 | tf_op jit(solution)/shard_map/ppermute | solution.py:236
  13.5 4.4 %collective-permute-start.1 = (bf16[4,7168]{1,0:T(4,128)(2,1)S(1)}, bf16[4,7168]{1,0:T(4,128)(2,1)S(1)}, u32[]{:S(2)}, u32[]{:S(2)}) collective-permute-start(bf16[4,7168]{1,0:T(4,128)(2,1)S(1)} %get-tuple-element.15.refs_0_), channel_id=1, source_target_pairs={{0,4},{1,5},{2,6},{3,7},{4,0},{5,1},{6,2},{7,3},{8,12},{9,13},{10,... | collective-permute-start | bytes 172040 | tf_op jit(solution)/shard_map/ppermute | solution.py:236
  14.3 5.2 %collective-permute-start.2 = (bf16[4,7168]{1,0:T(4,128)(2,1)S(1)}, bf16[4,7168]{1,0:T(4,128)(2,1)S(1)}, u32[]{:S(2)}, u32[]{:S(2)}) collective-permute-start(bf16[4,7168]{1,0:T(4,128)(2,1)S(1)} %get-tuple-element.15.refs_0_), channel_id=1, source_target_pairs={{0,6},{1,7},{2,4},{3,5},{4,2},{5,3},{6,0},{7,1},{8,14},{9,15},{10,... | collective-permute-start | bytes 172040 | tf_op jit(solution)/shard_map/ppermute | solution.py:236
  17.9 4.2 %collective-permute-start.4 = (bf16[4,7168]{1,0:T(4,128)(2,1)S(1)}, bf16[4,7168]{1,0:T(4,128)(2,1)S(1)}, u32[]{:S(2)}, u32[]{:S(2)}) collective-permute-start(bf16[4,7168]{1,0:T(4,128)(2,1)S(1)} %collective-permute-done.3.refs_4_), channel_id=1, source_target_pairs={{0,2},{1,3},{2,0},{3,1},{4,6},{5,7},{6,4},{7,5},{8,10},{9,11},{10,... | collective-permute-start | bytes 172040 | tf_op jit(solution)/shard_map/ppermute | solution.py:236
  19.5 4.8 %collective-permute-start.5 = (bf16[4,7168]{1,0:T(4,128)(2,1)S(1)}, bf16[4,7168]{1,0:T(4,128)(2,1)S(1)}, u32[]{:S(2)}, u32[]{:S(2)}) collective-permute-start(bf16[4,7168]{1,0:T(4,128)(2,1)S(1)} %collective-permute-done.3.refs_4_), channel_id=1, source_target_pairs={{0,4},{1,5},{2,6},{3,7},{4,0},{5,1},{6,2},{7,3},{8,12},{9,13},{10,... | collective-permute-start | bytes 172040 | tf_op jit(solution)/shard_map/ppermute | solution.py:236
  22.0 5.1 %collective-permute-start.6 = (bf16[4,7168]{1,0:T(4,128)(2,1)S(1)}, bf16[4,7168]{1,0:T(4,128)(2,1)S(1)}, u32[]{:S(2)}, u32[]{:S(2)}) collective-permute-start(bf16[4,7168]{1,0:T(4,128)(2,1)S(1)} %collective-permute-done.3.refs_4_), channel_id=1, source_target_pairs={{0,6},{1,7},{2,4},{3,5},{4,2},{5,3},{6,0},{7,1},{8,14},{9,15},{10,... | collective-permute-start | bytes 172040 | tf_op jit(solution)/shard_map/ppermute | solution.py:236
  27.1 1.5 %copy-start.2 = (bf16[1,7168,128]{2,1,0:T(8,128)(2,1)S(1)}, bf16[1,7168,128]{2,1,0:T(8,128)(2,1)}, u32[]{:S(2)}) copy-start(bf16[1,7168,128]{2,1,0:T(8,128)(2,1)} %param.13) | copy-start | bytes 5505028
  28.7 1.5 %copy-start.3 = (bf16[1,7168,128]{2,1,0:T(8,128)(2,1)S(1)}, bf16[1,7168,128]{2,1,0:T(8,128)(2,1)}, u32[]{:S(2)}) copy-start(bf16[1,7168,128]{2,1,0:T(8,128)(2,1)} %param.14) | copy-start | bytes 5505028
  34.5 6.0 %collective-permute-start.13 = (bf16[4,7168]{1,0:T(4,128)(2,1)S(1)}, bf16[4,7168]{1,0:T(4,128)(2,1)S(1)}, u32[]{:S(2)}, u32[]{:S(2)}) collective-permute-start(bf16[4,7168]{1,0:T(4,128)(2,1)S(1)} %get-tuple-element.21), channel_id=1, source_target_pairs={{0,2},{1,3},{2,0},{3,1},{4,6},{5,7},{6,4},{7,5},{8,10},{9,11},{10,... | collective-permute-start | bytes 172040 | tf_op jit(solution)/shard_map/ppermute | solution.py:236
  36.0 5.5 %collective-permute-start.14 = (bf16[4,7168]{1,0:T(4,128)(2,1)S(1)}, bf16[4,7168]{1,0:T(4,128)(2,1)S(1)}, u32[]{:S(2)}, u32[]{:S(2)}) collective-permute-start(bf16[4,7168]{1,0:T(4,128)(2,1)S(1)} %get-tuple-element.22), channel_id=1, source_target_pairs={{0,4},{1,5},{2,6},{3,7},{4,0},{5,1},{6,2},{7,3},{8,12},{9,13},{10,... | collective-permute-start | bytes 172040 | tf_op jit(solution)/shard_map/ppermute | solution.py:236
  37.0 5.7 %collective-permute-start.15 = (bf16[4,7168]{1,0:T(4,128)(2,1)S(1)}, bf16[4,7168]{1,0:T(4,128)(2,1)S(1)}, u32[]{:S(2)}, u32[]{:S(2)}) collective-permute-start(bf16[4,7168]{1,0:T(4,128)(2,1)S(1)} %get-tuple-element.23), channel_id=1, source_target_pairs={{0,6},{1,7},{2,4},{3,5},{4,2},{5,3},{6,0},{7,1},{8,14},{9,15},{10,... | collective-permute-start | bytes 172040 | tf_op jit(solution)/shard_map/ppermute | solution.py:236
  38.1 7.5 %collective-permute-start.10 = (bf16[4,7168]{1,0:T(4,128)(2,1)S(1)}, bf16[4,7168]{1,0:T(4,128)(2,1)S(1)}, u32[]{:S(2)}, u32[]{:S(2)}) collective-permute-start(bf16[4,7168]{1,0:T(4,128)(2,1)S(1)} %get-tuple-element.17), channel_id=1, source_target_pairs={{0,2},{1,3},{2,0},{3,1},{4,6},{5,7},{6,4},{7,5},{8,10},{9,11},{10,... | collective-permute-start | bytes 172040 | tf_op jit(solution)/shard_map/ppermute | solution.py:236
  39.5 6.1 %collective-permute-start.11 = (bf16[4,7168]{1,0:T(4,128)(2,1)S(1)}, bf16[4,7168]{1,0:T(4,128)(2,1)S(1)}, u32[]{:S(2)}, u32[]{:S(2)}) collective-permute-start(bf16[4,7168]{1,0:T(4,128)(2,1)S(1)} %get-tuple-element.18), channel_id=1, source_target_pairs={{0,4},{1,5},{2,6},{3,7},{4,0},{5,1},{6,2},{7,3},{8,12},{9,13},{10,... | collective-permute-start | bytes 172040 | tf_op jit(solution)/shard_map/ppermute | solution.py:236
  40.5 5.1 %collective-permute-start.12 = (bf16[4,7168]{1,0:T(4,128)(2,1)S(1)}, bf16[4,7168]{1,0:T(4,128)(2,1)S(1)}, u32[]{:S(2)}, u32[]{:S(2)}) collective-permute-start(bf16[4,7168]{1,0:T(4,128)(2,1)S(1)} %get-tuple-element.19), channel_id=1, source_target_pairs={{0,6},{1,7},{2,4},{3,5},{4,2},{5,3},{6,0},{7,1},{8,14},{9,15},{10,... | collective-permute-start | bytes 172040 | tf_op jit(solution)/shard_map/ppermute | solution.py:236
  42.7 5.8 %collective-permute-start.16 = (bf16[4,7168]{1,0:T(4,128)(2,1)S(1)}, bf16[4,7168]{1,0:T(4,128)(2,1)S(1)}, u32[]{:S(2)}, u32[]{:S(2)}) collective-permute-start(bf16[4,7168]{1,0:T(4,128)(2,1)S(1)} %add_convert_fusion), channel_id=1, source_target_pairs={{0,8},{1,9},{2,10},{3,11},{4,12},{5,13},{6,14},{7,15},{8,0},{9,1},... | collective-permute-start | bytes 172040 | tf_op jit(solution)/shard_map/ppermute | solution.py:236
